TPU v7x, 256 devices: a whole 4x4x8 slice. The times are simulated.
256 devices in a mesh: major: 16 (over x, y), minor: 16 (over z, core).
Axes of the slice: x: 4, y: 4, z: 8, core: 2. Of those that a mesh axis runs over, the one named last changes fastest.
Arguments:
- context: bfloat16 [131072, 1024], P(('major', 'minor')), may hold values from -100 to 100
- latents: bfloat16 [2048, 1024], P('major'), may hold values from -6 to 6
- ends: int32 [2048], replicated, may hold values from 1 to 131072, as said below
- w_query: bfloat16 [1024, 1024], replicated, may hold values from -2 to 2
- w_key: bfloat16 [1024, 1024], replicated, may hold values from -1 to 1
- w_value: bfloat16 [1024, 1024], replicated, may hold values from -0.1875 to 0.1875
- w_out: bfloat16 [1024, 1024], P('minor'), may hold values from -1.5 to 1.5
Outputs:
- mixed: bfloat16 [2048, 1024], P(('major', 'minor'))
Inputs may be any that keep to these rules, and one draw needn't show every extreme that they name: Latent row q attends context positions 0 to ends[q] - 1.
All inputs are finite; a program needn't handle non-finite values.
Results may differ from a plain program's by a relative error of at most 0.015.
The roundings to bfloat16 on the way count: a program that leaves them out, or rounds other values in their place, can miss the bound.
Values may be sent and summed in bfloat16 or wider, within the bound.
A program may use at most 128 MiB of HBM per device.

v0:
```python
import jax
import jax.numpy as jnp
from jax import lax
from jax.sharding import PartitionSpec as P

HEAD = 64


def block_terms(query_block, keys, values, limit_block, start):
    count = keys.shape[0]
    heads = query_block.shape[1]
    key_heads = keys.reshape(count, heads, -1)
    value_heads = values.reshape(count, heads, -1)
    scores = jnp.einsum("qhd,khd->qhk", query_block, key_heads, preferred_element_type=jnp.float32)
    places = start + jnp.arange(count, dtype=jnp.int32)
    live = places[None, :] < limit_block[:, None]
    scores = jnp.where(live[:, None, :], scores, -1e30)
    block_max = jnp.max(scores, axis=2)
    expon = jnp.exp(scores - block_max[:, :, None])
    block_sum = jnp.sum(expon, axis=2)
    probs = expon.astype(jnp.bfloat16)
    block_out = jnp.einsum("qhk,khd->qhd", probs, value_heads, preferred_element_type=jnp.float32)
    return (block_max, block_sum, block_out)


def local(context, latents, ends, w_query, w_key, w_value, w_out):
    tok_rows = context.shape[0]
    width = context.shape[1]
    keys = jnp.dot(context, w_key, preferred_element_type=jnp.float32).astype(jnp.bfloat16)
    values = jnp.dot(context, w_value, preferred_element_type=jnp.float32).astype(jnp.bfloat16)
    own_queries = (
        jnp.dot(latents, w_query, preferred_element_type=jnp.float32) * HEAD ** (-0.5)
    ).astype(jnp.bfloat16)
    queries = lax.all_gather(own_queries, "major", axis=0, tiled=True)
    total_rows = queries.shape[0]
    heads = width // HEAD
    block_rows = min(512, total_rows)
    nblocks = total_rows // block_rows
    n_major = lax.axis_size("major")
    own_rows = total_rows // n_major
    limit_blocks = ends.reshape(nblocks, block_rows)

    def one_block(item):
        query_block, limit_block = item
        return block_terms(
            query_block, keys, values, limit_block, lax.axis_index(("major", "minor")) * tok_rows
        )

    block_max, block_sum, block_out = lax.map(
        one_block, (queries.reshape(nblocks, block_rows, heads, HEAD), limit_blocks)
    )
    block_max = block_max.reshape(total_rows, heads)
    block_sum = block_sum.reshape(total_rows, heads)
    block_out = block_out.reshape(total_rows, heads, HEAD)
    top = lax.pmax(block_max.astype(jnp.bfloat16), ("major", "minor")).astype(block_max.dtype)
    factor = jnp.exp(block_max - top)
    numerator = (block_out * factor[:, :, None]).reshape(total_rows, width)
    denominator = block_sum * factor
    by_heads = (
        lax.psum_scatter(numerator, "minor", scatter_dimension=1, tiled=True),
        lax.psum_scatter(denominator, "minor", scatter_dimension=1, tiled=True),
    )
    num_own, den_own = (
        lax.psum_scatter(by_heads[0], "major", scatter_dimension=0, tiled=True),
        lax.psum_scatter(by_heads[1], "major", scatter_dimension=0, tiled=True),
    )
    kept_heads = den_own.shape[1]
    attended = (num_own.reshape(own_rows, kept_heads, HEAD) / den_own[:, :, None]).reshape(
        own_rows, kept_heads * HEAD
    )
    attended = attended.astype(jnp.bfloat16)
    mixed = lax.psum_scatter(
        jnp.dot(attended, w_out, preferred_element_type=jnp.float32),
        "minor",
        scatter_dimension=0,
        tiled=True,
    )
    return mixed.astype(jnp.bfloat16)


def solution(mesh):
    in_specs = (P(("major", "minor"), None), P("major", None), P(), P(), P(), P(), P("minor", None))
    out_specs = P(("major", "minor"), None)
    return jax.shard_map(local, mesh=mesh, in_specs=in_specs, out_specs=out_specs, check_vma=False)
```

profile of v0, /device:TPU:17, one launch (start us, length us, event | category | flops | bytes accessed | tf_op | source)
XLA Modules:
  0.0 1017.4 jit_solution(9159840516394256270)
XLA Ops:
  17.9 51.2 %all-gather.2.cloned.1.call-done = bf16[2048,1024]{1,0:T(8,128)(2,1)} async-done(((bf16[128,1024]{1,0:T(8,128)(2,1)}), bf16[2048,1024]{1,0:T(8,128)(2,1)}) %all-gather.2.cloned.1.call-update) | async-done | bytes 4194320 | tf_op jit(solution)/shard_map/all_gather | solution.py:34
  69.1 11.6 %reshape.69 = bf16[4,512,16,64]{3,2,1,0:T(8,128)(2,1)} reshape(bf16[2048,1024]{1,0:T(8,128)(2,1)} %all-gather.2.cloned.1.call-done) | data formatting | bytes 8388608 | tf_op jit(solution)/shard_map/reshape | solution.py:50
  80.7 9.7 copy.23
  90.4 284.3 %while.14 = (s32[]{:T(128)}, f32[4,512,16]{1,0,2:T(4,128)S(1)}, f32[4,512,16]{1,0,2:T(4,128)S(1)}, f32[4,512,16,64]{1,0,3,2:T(4,128)}, s32[4,512]{1,0:T(4,128)S(...) while((s32[]{:T(128)}, f32[4,512,16]{1,0,2:T(4,128)S(1)}, ...), condition=%wide.region_3.4_spmd, body=%wide.region_0.3_spmd.sunk | while | flops 1107542528 | bytes 65415420 | solution.py:49
  90.7 9.4 bitcast_reduce_fusion.2
  100.3 8.7 fusion.37
  109.2 7.9 fusion.38
  120.6 41.0 %dynamic_update_slice.16 = f32[4,512,16,64]{1,0,3,2:T(4,128)} dynamic-update-slice(f32[4,512,16,64]{1,0,3,2:T(4,128)} %get-tuple-element.166, f32[1,512,16,64]{1,0,3,2:T(1,128)} %copy.48, s32[]{:T(128)S(6)} %copy.56, s32[]{:T(128)} %constant.35.clone.1..sunk, s32[]{:T(128)} %constant.35.clone.1..sunk, s32[]{:T(128)} %constant.35.clone.1..sunk) | dynamic-update-slice | bytes 4194308 | tf_op jit(solution)/shard_map/while/body/jit(dynamic_update_index_in_dim)/dynamic_update_slice | solution.py:49
  161.8 9.4 bitcast_reduce_fusion.2
  171.4 8.7 fusion.37
  191.7 41.0 %dynamic_update_slice.16 = f32[4,512,16,64]{1,0,3,2:T(4,128)} dynamic-update-slice(f32[4,512,16,64]{1,0,3,2:T(4,128)} %get-tuple-element.166, f32[1,512,16,64]{1,0,3,2:T(1,128)} %copy.48, s32[]{:T(128)S(6)} %copy.56, s32[]{:T(128)} %constant.35.clone.1..sunk, s32[]{:T(128)} %constant.35.clone.1..sunk, s32[]{:T(128)} %constant.35.clone.1..sunk) | dynamic-update-slice | bytes 4194308 | tf_op jit(solution)/shard_map/while/body/jit(dynamic_update_index_in_dim)/dynamic_update_slice | solution.py:49
  232.9 9.4 bitcast_reduce_fusion.2
  242.5 8.7 fusion.37
  262.7 41.0 %dynamic_update_slice.16 = f32[4,512,16,64]{1,0,3,2:T(4,128)} dynamic-update-slice(f32[4,512,16,64]{1,0,3,2:T(4,128)} %get-tuple-element.166, f32[1,512,16,64]{1,0,3,2:T(1,128)} %copy.48, s32[]{:T(128)S(6)} %copy.56, s32[]{:T(128)} %constant.35.clone.1..sunk, s32[]{:T(128)} %constant.35.clone.1..sunk, s32[]{:T(128)} %constant.35.clone.1..sunk) | dynamic-update-slice | bytes 4194308 | tf_op jit(solution)/shard_map/while/body/jit(dynamic_update_index_in_dim)/dynamic_update_slice | solution.py:49
  303.9 9.4 bitcast_reduce_fusion.2
  313.6 8.7 fusion.37
  322.5 7.9 fusion.38
  333.8 41.0 %dynamic_update_slice.16 = f32[4,512,16,64]{1,0,3,2:T(4,128)} dynamic-update-slice(f32[4,512,16,64]{1,0,3,2:T(4,128)} %get-tuple-element.166, f32[1,512,16,64]{1,0,3,2:T(1,128)} %copy.48, s32[]{:T(128)S(6)} %copy.56, s32[]{:T(128)} %constant.35.clone.1..sunk, s32[]{:T(128)} %constant.35.clone.1..sunk, s32[]{:T(128)} %constant.35.clone.1..sunk) | dynamic-update-slice | bytes 4194308 | tf_op jit(solution)/shard_map/while/body/jit(dynamic_update_index_in_dim)/dynamic_update_slice | solution.py:49
  375.6 237.0 %all-reduce.4.cloned.1.call-done = bf16[2048,16]{0,1:T(8,128)(2,1)} async-done(((bf16[2048,16]{0,1:T(8,128)(2,1)}), bf16[2048,16]{0,1:T(8,128)(2,1)}) %all-reduce.4.cloned.1.call-update) | async-done | bytes 65552 | tf_op jit(solution)/shard_map/pmax | solution.py:55
  627.3 92.2 %all-reduce.6.cloned.1.call-done = f32[2048,16]{0,1:T(8,128)} async-done(((f32[2048,16]{0,1:T(8,128)}), f32[2048,16]{0,1:T(8,128)}) %all-reduce.6.cloned.1.call-update) | async-done | bytes 131088
  722.5 67.6 %reduce-scatter.7.cloned.1.call-done = f32[2048,64]{0,1:T(8,128)} async-done(((f32[2048,1024]{0,1:T(8,128)}), f32[2048,64]{0,1:T(8,128)}) %reduce-scatter.7.cloned.1.call-update) | async-done | bytes 524304 | tf_op jit(solution)/shard_map/reduce_scatter | solution.py:60
  790.2 80.7 %reduce-scatter.13.cloned.1.call-done = f32[128,1]{1,0:T(8,128)} async-done(((f32[2048,1]{1,0:T(8,128)}), f32[128,1]{1,0:T(8,128)}) %reduce-scatter.13.cloned.1.call-update) | async-done | bytes 528
  871.8 79.1 %reduce-scatter.9.cloned.1.call-done = f32[128,64]{0,1:T(8,128)} async-done(((f32[2048,64]{0,1:T(8,128)}), f32[128,64]{0,1:T(8,128)}) %reduce-scatter.9.cloned.1.call-update) | async-done | bytes 32784 | tf_op jit(solution)/shard_map/reduce_scatter | solution.py:64
  952.7 56.5 %reduce-scatter.11.cloned.1.call-done = f32[8,1024]{1,0:T(8,128)} async-done(((f32[128,1024]{1,0:T(8,128)}), f32[8,1024]{1,0:T(8,128)}) %reduce-scatter.11.cloned.1.call-update) | async-done | bytes 32784 | tf_op jit(solution)/shard_map/reduce_scatter | solution.py:72
  (77 shorter events, 66.1 us)
Async XLA Ops:
  6.5 3.8 copy-start
  6.5 62.6 %all-gather.2.cloned.1.call-start = ((), (), s32[]{:S(2)}) async-start(), calls=%async_computation.4 | async-start | bytes 4456448 | tf_op jit(solution)/shard_map/all_gather | solution.py:34
  9.5 603.1 %all-reduce.4.cloned.1.call-start = ((), (), s32[]{:S(2)}) async-start(), calls=%async_computation.5 | async-start | bytes 131072 | tf_op jit(solution)/shard_map/pmax | solution.py:55
  375.5 344.0 %all-reduce.6.cloned.1.call-start = ((), (), s32[]{:S(2)}) async-start(), calls=%async_computation.10 | async-start | bytes 262144
  614.1 176.0 %reduce-scatter.7.cloned.1.call-start = ((), (), s32[]{:S(2)}) async-start(), calls=%async_computation.6 | async-start | bytes 8912896 | tf_op jit(solution)/shard_map/reduce_scatter | solution.py:60
  621.9 388.7 %copy-start.1 = (bf16[1024,1024]{1,0:T(8,128)(2,1)S(1)}, bf16[1024,1024]{1,0:T(8,128)(2,1)}, u32[]{:S(2)}) copy-start(bf16[1024,1024]{1,0:T(8,128)(2,1)} %param.13) | copy-start | bytes 6291460
  626.1 0.7 copy-start.3
  626.1 324.8 %copy-start.2 = (bf16[64,1024]{1,0:T(8,128)(2,1)S(1)}, bf16[64,1024]{1,0:T(8,128)(2,1)}, u32[]{:S(2)}) copy-start(bf16[64,1024]{1,0:T(8,128)(2,1)} %param.15) | copy-start | bytes 393220
  626.1 244.8 %reduce-scatter.13.cloned.1.call-start = ((), (), s32[]{:S(2)}) async-start(), calls=%async_computation.9 | async-start | bytes 1114112
  722.5 228.4 %reduce-scatter.9.cloned.1.call-start = ((), (), s32[]{:S(2)}) async-start(), calls=%async_computation.7 | async-start | bytes 557056 | tf_op jit(solution)/shard_map/reduce_scatter | solution.py:64
  790.1 219.1 %reduce-scatter.11.cloned.1.call-start = ((), (), s32[]{:S(2)}) async-start(), calls=%async_computation.8 | async-start | bytes 557056 | tf_op jit(solution)/shard_map/reduce_scatter | solution.py:72
Sparse Core Ops, SparseCore 0:
  9.8 59.2 all-gather.1
  375.6 236.9 all-reduce.3
  614.9 104.5 all-reduce.5
  722.1 67.9 reduce-scatter.6
  793.8 76.9 reduce-scatter.12
  874.2 76.6 reduce-scatter.8
  953.6 55.6 reduce-scatter.10
where the time goes:
time: 1030 us; the launch traced here: 1020 us
  waiting for transfers between devices  664 us (64%)
  local copies, waits for them, and re-layouts  216 us (21%)
  matrix products  79.6 us (8%)
  other arithmetic  43.2 us (4%)
  between operations  13.6 us (1%)
    pmax x1, waiting for transfers between devices, local(): lax.pmax(block_max.astype(jnp.bfloat16), ('major', 'minor'))  237 us
    dynamic_update_slice x24, local copies, waits for them, and re-layouts, local(): lax.map(one_block, (queries.reshape(nblocks, block_rows, heads, HEAD), li...  179 us
    unnamed x9, waiting for transfers between devices  173 us
    reduce_scatter x1, waiting for transfers between devices, local(): lax.psum_scatter(by_heads[0], 'major', scatter_dimension=0, tiled=True)  79.1 us
    reduce_scatter x1, waiting for transfers between devices, local(): lax.psum_scatter(numerator, 'minor', scatter_dimension=1, tiled=True)  67.6 us
    reduce_scatter x1, waiting for transfers between devices, local(): lax.psum_scatter(jnp.dot(attended, w_out, preferred_element_type=jnp.floa...  56.5 us
    all_gather x1, waiting for transfers between devices, local(): queries = lax.all_gather(own_queries, 'major', axis=0, tiled=True)  51.2 us
    dot_general x4, matrix products, block_terms(): jnp.einsum('qhd,khd->qhk', query_block, key_heads, preferred_element_type...  37.7 us
  transfers between devices with their start and end apart: 7, of which 7 were waited for; matrix products, arithmetic and copies ran while one was open for 2% of the time, Pallas kernels for 0%

commit v1 on v0

v1 whole, which is shorter than its diff:
```python
import math

import jax
import jax.numpy as jnp
from jax import lax
from jax.experimental import pallas as pl
from jax.experimental.pallas import tpu as pltpu
from jax.sharding import PartitionSpec as P

HEAD = 64
NX, NY, NZ = 4, 4, 8
HEADS = 8
FEAT = HEADS * HEAD
PHASES = 2
GROUP = HEADS // PHASES
WIDE = GROUP * HEAD
TOK = 512
POS = 2 * TOK
ROWS = 128
OWN = 2 * 8
VROWS = 80
PAY = WIDE + 32
LOG2E = math.log2(math.e)
NEG = -1e30
MESH = pl.DeviceIdType.MESH
BF = jnp.bfloat16
F32 = jnp.float32


def split3(a):
    hi = a.astype(BF)
    rest = a - hi.astype(F32)
    mid = rest.astype(BF)
    low = (rest - mid.astype(F32)).astype(BF)
    return hi, mid, low


def stats_of(pay):
    rows = pay[WIDE:, :].astype(F32)
    return rows[:8] + rows[8:16] + rows[16:24]


def stats_rows(stats):
    terms = [t.astype(F32) for t in split3(stats)]
    return jnp.concatenate(terms + [jnp.zeros_like(stats)], axis=0)


def merge(pays):
    stats = [stats_of(pay) for pay in pays]
    top = stats[0][:GROUP]
    for st in stats[1:]:
        top = jnp.maximum(top, st[:GROUP])
    factors = [jnp.exp2(st[:GROUP] - top) for st in stats]
    den = sum(f * st[GROUP:] for f, st in zip(factors, stats))
    nums = []
    for h in range(GROUP):
        rows = slice(h * HEAD, h * HEAD + HEAD)
        nums.append(sum(pay[rows, :].astype(F32) * f[h : h + 1, :] for f, pay in zip(factors, pays)))
    return nums, jnp.concatenate([top, den], axis=0)


def write_payload(dst, nums, stats):
    for h in range(GROUP):
        dst[h * HEAD : h * HEAD + HEAD, :] = nums[h].astype(BF)
    dst[WIDE:, :] = stats_rows(stats).astype(BF)


def kernel(
    ctx_ref, lat_ref, ends_ref, wq_ref, wk_ref, wv_ref, wo_ref, out_ref,
    ctx, lat, wq, wk, wv, wo, qt, kk, vt, part, recv_x, sum_y, recv_y, zsend, zbuf, mix, mix_in, first_scores,
    load_sem, ctx_sem, wo_send, wo_recv, qx_send, qd_send, qy_send, q_recv,
    x_send, x_recv, y_send, y_recv, z_send, z_recv, core_sem,
):
    major, minor = lax.axis_index("major"), lax.axis_index("minor")
    x, y = lax.div(major, NY), lax.rem(major, NY)
    z, c = lax.div(minor, 2), lax.rem(minor, 2)

    def at_x(d):
        return (lax.rem(x + d, NX) * NY + y, minor)

    def at_y(d):
        return (x * NY + lax.rem(y + d, NY), minor)

    def at_xy(d, e):
        return (lax.rem(x + d, NX) * NY + lax.rem(y + e, NY), minor)

    other = (major, 2 * z + 1 - c)
    half = pl.ds(pl.multiple_of(c * FEAT, FEAT), FEAT)
    mine = pl.ds(pl.multiple_of(c * TOK, TOK), TOK)
    theirs = pl.ds(pl.multiple_of((1 - c) * TOK, TOK), TOK)

    loads = [
        pltpu.make_async_copy(lat_ref, lat, load_sem.at[0]),
        pltpu.make_async_copy(wq_ref.at[:, half], wq, load_sem.at[1]),
        pltpu.make_async_copy(ctx_ref, ctx.at[mine], load_sem.at[2]),
        pltpu.make_async_copy(wk_ref.at[:, half], wk, load_sem.at[3]),
        pltpu.make_async_copy(wv_ref.at[:, half], wv, load_sem.at[4]),
    ]
    for load in loads:
        load.start()

    barrier = pltpu.get_barrier_semaphore()
    for d in range(1, 4):
        pl.semaphore_signal(barrier, inc=1, device_id=at_x(d), device_id_type=MESH)
        pl.semaphore_signal(barrier, inc=1, device_id=at_y(d), device_id_type=MESH)
    for d in (1, 3):
        for e in (1, 3):
            pl.semaphore_signal(barrier, inc=1, device_id=at_xy(d, e), device_id_type=MESH)
    for d in range(1, 16):
        pl.semaphore_signal(barrier, inc=1, device_id=(major, lax.rem(minor + d, 16)), device_id_type=MESH)
    pl.semaphore_wait(barrier, 25)

    ctx_copy = pltpu.make_async_remote_copy(
        src_ref=ctx_ref, dst_ref=ctx.at[mine], send_sem=ctx_sem.at[0], recv_sem=ctx_sem.at[1],
        device_id=other, device_id_type=MESH,
    )
    ctx_copy.start()

    def q_block(xx, yy):
        return xx * NY + yy

    own = q_block(x, y)
    loads[0].wait()
    loads[1].wait()
    q = jnp.dot(lat[...], wq[...], preferred_element_type=F32) * HEAD ** (-0.5)
    q = jnp.transpose(q.astype(BF).astype(F32)).astype(BF)
    for g in range(PHASES):
        qt[g, own] = q[g * WIDE : (g + 1) * WIDE, :]

    def q_copy(g, block, send_sem, device):
        return pltpu.make_async_remote_copy(
            src_ref=qt.at[g, block], dst_ref=qt.at[g, block], send_sem=send_sem, recv_sem=q_recv.at[g, block],
            device_id=device, device_id_type=MESH,
        )

    def q_along_x(g, d):
        return q_copy(g, own, qx_send.at[g, d - 1], at_x(NX - d))

    def q_along_y(g, dx, d):
        return q_copy(g, q_block(lax.rem(x + dx, NX), y), qy_send.at[g, dx, d - 1], at_y(NY - d))

    def q_across(i, d):
        return q_copy(0, own, qd_send.at[i], at_xy(d, NY - 1))

    def q_wait(g, xx, yy):
        q_copy(g, q_block(xx, yy), qx_send.at[0, 0], other).wait_recv()

    q_along_y(0, 0, 1).start()
    q_along_x(0, 1).start()
    q_along_x(0, 3).start()
    q_across(0, 3).start()
    q_across(1, 1).start()
    q_along_y(0, 0, 2).start()
    q_along_y(0, 0, 3).start()
    q_along_x(0, 2).start()

    lane = lax.broadcasted_iota(jnp.int32, (TOK, 128), 1)

    def project_keys(rows):
        keys = jnp.dot(ctx[rows, :], wk[...], preferred_element_type=F32).astype(BF).astype(F32) * LOG2E
        hi = keys.astype(BF).astype(F32)
        low = (keys - hi).astype(BF).astype(F32)
        for pair in range(HEADS // 2):
            cols = slice(pair * 128, pair * 128 + 128)
            a, b = hi[:, cols], low[:, cols]
            even = jnp.where(lane < HEAD, a, pltpu.roll(b, HEAD, 1))
            odd = jnp.where(lane < HEAD, pltpu.roll(a, HEAD, 1), b)
            g, start = divmod(2 * pair, GROUP)
            kk[g, rows, start * 128 : start * 128 + 128] = even.astype(BF)
            kk[g, rows, start * 128 + 128 : start * 128 + 256] = odd.astype(BF)

    def project_values(rows):
        values = jnp.dot(ctx[rows, :], wv[...], preferred_element_type=F32).astype(BF).astype(F32)
        turned = jnp.transpose(values).astype(BF)
        for h in range(HEADS):
            g, i = divmod(h, GROUP)
            vt[g, i * VROWS : i * VROWS + HEAD, rows] = turned[h * HEAD : h * HEAD + HEAD, :]

    loads[2].wait()
    loads[3].wait()
    project_keys(mine)


    group, place = lax.div(minor, HEADS), lax.rem(minor, HEADS)
    wo_rows = pl.ds(pl.multiple_of(place * HEAD, HEAD), HEAD)

    def wo_copy(dz):
        return pltpu.make_async_remote_copy(
            src_ref=wo_ref, dst_ref=wo.at[wo_rows], send_sem=wo_send.at[dz], recv_sem=wo_recv.at[place],
            device_id=(major, lax.rem(z + dz, NZ) * 2 + group), device_id_type=MESH,
        )

    wo_local = pltpu.make_async_copy(wo_ref, wo.at[wo_rows], wo_recv.at[place])
    for dz in range(1, NZ):
        wo_copy(dz).start()

    @pl.when(c == group)
    def _():
        wo_local.start()

    @pl.when(c != group)
    def _():
        wo_copy(0).start()

    loads[4].wait()
    project_values(mine)
    row16 = lax.broadcasted_iota(jnp.int32, (16, POS), 0)
    for h in range(HEADS):
        g, i = divmod(h, GROUP)
        vt[g, i * VROWS + HEAD : (i + 1) * VROWS, :] = jnp.where(row16 == 0, 1.0, 0.0).astype(BF)

    ctx_copy.wait()
    project_keys(theirs)
    project_values(theirs)

    def x_copy(g, dx, yy):
        return pltpu.make_async_remote_copy(
            src_ref=part.at[g, q_block(lax.rem(x + dx, NX), yy)], dst_ref=recv_x.at[g, dx - 1, yy],
            send_sem=x_send.at[g, dx - 1, yy], recv_sem=x_recv.at[g, dx - 1, yy],
            device_id=at_x(dx), device_id_type=MESH,
        )

    def y_copy(g, dy):
        return pltpu.make_async_remote_copy(
            src_ref=sum_y.at[g, dy - 1], dst_ref=recv_y.at[g, dy - 1], send_sem=y_send.at[g, dy - 1],
            recv_sem=y_recv.at[g, dy - 1], device_id=at_y(dy), device_id_type=MESH,
        )

    def add_along_x(g, dy):
        yy = lax.rem(y + dy, NY)
        for d in range(1, 4):
            x_copy(g, d, yy).wait_recv()
        write_payload(sum_y.at[g, dy - 1], *merge([part.at[g, q_block(x, yy)]] + [recv_x.at[g, d, yy] for d in range(3)]))
        y_copy(g, dy).start()

    def z_rows(dz):
        return pl.ds(pl.multiple_of(lax.rem(z + dz, NZ) * OWN, OWN), OWN)

    def z_copy(g, dz):
        return pltpu.make_async_remote_copy(
            src_ref=zsend.at[g, z_rows(dz)], dst_ref=zbuf.at[g, z], send_sem=z_send.at[g, dz],
            recv_sem=z_recv.at[g, z], device_id=(major, lax.rem(z + dz, NZ) * 2 + c), device_id_type=MESH,
        )

    def add_along_y(g):
        for d in range(1, 4):
            x_copy(g, d, y).wait_recv()
        for d in range(1, 4):
            y_copy(g, d).wait_recv()
        nums, stats = merge(
            [part.at[g, own]] + [recv_x.at[g, d, y] for d in range(3)] + [recv_y.at[g, d] for d in range(3)]
        )
        zsend[g, :, :WIDE] = jnp.transpose(jnp.concatenate(nums, axis=0)).astype(BF)
        rows = jnp.concatenate([stats_rows(stats), jnp.zeros((96, ROWS), F32)], axis=0)
        zsend[g, :, WIDE:] = jnp.transpose(rows).astype(BF)
        for dz in range(1, NZ):
            z_copy(g, dz).start()
        pltpu.make_async_copy(zsend.at[g, z_rows(0)], zbuf.at[g, z], z_recv.at[g, z]).start()

    def add_along_z(g):
        head_of = lax.shift_right_logical(lax.broadcasted_iota(jnp.int32, (128, WIDE), 1), 6)
        line = lax.broadcasted_iota(jnp.int32, (128, WIDE), 0)
        spread = jnp.where(head_of == line, 1.0, 0.0).astype(BF)
        spread_den = jnp.where(head_of == line - GROUP, 1.0, 0.0).astype(BF)
        lane16 = lax.broadcasted_iota(jnp.int32, (OWN, 128), 1)
        for i in range(NZ):
            pltpu.make_async_copy(zsend.at[g, pl.ds(0, OWN)], zbuf.at[g, i], z_recv.at[g, i]).wait()
        sums = []
        for i in range(NZ):
            t = zbuf[g, i, :, WIDE:].astype(F32)
            sums.append(t + pltpu.roll(t, 120, 1) + pltpu.roll(t, 112, 1))
        top = sums[0]
        for t in sums[1:]:
            top = jnp.maximum(top, t)
        factors = [jnp.where(lane16 < GROUP, jnp.exp2(t - top), 0.0) for t in sums]
        wide = jnp.dot(jnp.concatenate(factors, axis=0).astype(BF), spread, preferred_element_type=F32)
        num = sum(wide[i * OWN : i * OWN + OWN] * zbuf[g, i, :, :WIDE].astype(F32) for i in range(NZ))
        den = sum(pltpu.roll(f, GROUP, 1) * t for f, t in zip(factors, sums))
        den_wide = sum(jnp.dot(t, spread_den, preferred_element_type=F32) for t in split3(den))
        attended = (num / den_wide).astype(BF)
        return jnp.dot(attended, wo[g * WIDE : (g + 1) * WIDE, :], preferred_element_type=F32)

    def wo_wait(i):
        pltpu.make_async_copy(wo_ref, wo.at[pl.ds(i * HEAD, HEAD)], wo_recv.at[i]).wait()

    base = (major * 16 + 2 * z) * TOK
    place_in_pos = lax.broadcasted_iota(jnp.int32, (POS, 2 * ROWS), 0)

    def scores(g, blocks, h):
        rows = slice(h * HEAD, h * HEAD + HEAD)
        qh = jnp.concatenate([qt[g, b, rows, :] for b in blocks], axis=1)
        qh = jnp.concatenate([qh, qh], axis=0)
        return jnp.dot(kk[g, :, h * 128 : h * 128 + 128], qh, preferred_element_type=F32)

    def attend(g, blocks, next_g, next_blocks):
        ends = jnp.concatenate([ends_ref[pl.ds(b, 1), :] for b in blocks], axis=1) - base
        live = place_in_pos < ends
        tops, dens = [], []
        ahead = first_scores[...]
        for h in range(GROUP):
            now = ahead
            if h + 1 < GROUP:
                ahead = scores(g, blocks, h + 1)
            else:
                first_scores[...] = scores(next_g, next_blocks, 0)
            now = jnp.where(live, now, NEG)
            top = jnp.ceil(jnp.max(now, axis=0, keepdims=True))
            probs = jnp.exp2(now - top).astype(BF)
            res = jnp.dot(vt[g, h * VROWS : (h + 1) * VROWS, :], probs, preferred_element_type=F32)
            for i, b in enumerate(blocks):
                part[g, b, h * HEAD : h * HEAD + HEAD, :] = res[:HEAD, i * ROWS : i * ROWS + ROWS].astype(BF)
            tops.append(top)
            dens.append(res[HEAD : HEAD + 1, :])
        rows = stats_rows(jnp.concatenate(tops + dens, axis=0)).astype(BF)
        for i, b in enumerate(blocks):
            part[g, b, WIDE:, :] = rows[:, i * ROWS : i * ROWS + ROWS]

    def plan(it):
        g, s = lax.div(it, 8), lax.rem(it, 8)
        early = jnp.where(g == 0, s < 2, s >= 6)
        t = jnp.where(g == 0, s + 4, s)
        k, second = lax.rem(t, 3), jnp.where(g == 0, lax.div(t - 6, 3), lax.div(t, 3))
        dx = jnp.where(g == 0, jnp.where(k == 2, 2, 1 + 2 * k), jnp.where(k == 0, 2, 2 * k - 1))
        dx = jnp.where(early, 0, dx)
        second = jnp.where(early, lax.rem(s, 2), second)
        xx = lax.rem(x + dx, NX)
        first = 2 * second + g
        dys = [first, lax.rem(first + 1, NY)]
        yys = [lax.rem(y + dy, NY) for dy in dys]
        return g, dx, xx, dys, yys

    def wait_queries(g, xx, dys, yys):
        for dy, yy in zip(dys, yys):

            @pl.when(dy != 0)
            def _():
                q_wait(g, xx, yy)

    def step(it, carry):
        g, dx, xx, dys, yys = plan(it)
        next_g, _, next_xx, next_dys, next_yys = plan(jnp.minimum(it + 1, 8 * PHASES - 1))

        @pl.when(it == 0)
        def _():
            for dx in (2, 1, 3):
                q_wait(0, lax.rem(x + dx, NX), y)
                for d in range(1 if dx == 2 else 2, 4):
                    q_along_y(0, dx, d).start()
            for d in (2, 1, 3):
                q_along_x(1, d).start()

        @pl.when(it == 3)
        def _():
            for dx in (2, 1, 3):
                q_wait(1, lax.rem(x + dx, NX), y)
                for d in range(1, 4):
                    q_along_y(1, dx, d).start()

        @pl.when(it == 5)
        def _():
            for d in range(1, 4):
                q_along_y(1, 0, d).start()

        @pl.when(it + 1 < 8 * PHASES)
        def _():
            wait_queries(next_g, next_xx, next_dys, next_yys)

        attend(g, [q_block(xx, yy) for yy in yys], next_g, [q_block(next_xx, yy) for yy in next_yys])

        @pl.when(dx != 0)
        def _():
            for yy in yys:
                x_copy(g, dx, yy).start()

        @pl.when((it == 9) | (it == 14))
        def _():
            for dy in (1, 2):
                add_along_x(lax.div(it - 9, 5), dy)

        @pl.when(it == 9)
        def _():
            add_along_x(0, 3)

        @pl.when(it == 13)
        def _():
            add_along_y(0)

        return carry

    q_wait(0, x, lax.rem(y + 1, NY))
    first_scores[...] = scores(0, [own, q_block(x, lax.rem(y + 1, NY))], 0)
    lax.fori_loop(0, 8 * PHASES, step, 0)

    add_along_x(1, 3)
    for i in range(HEADS):
        wo_wait(i)
    mix[...] = add_along_z(0)
    add_along_y(1)
    mix[...] += add_along_z(1)
    core_copy = pltpu.make_async_remote_copy(
        src_ref=mix.at[pl.ds(pl.multiple_of((1 - c) * 8, 8), 8)], dst_ref=mix_in,
        send_sem=core_sem.at[0], recv_sem=core_sem.at[1], device_id=other, device_id_type=MESH,
    )
    core_copy.start()

    q_across(0, 3).wait_send()
    q_across(1, 1).wait_send()
    for g in range(PHASES):
        for d in range(1, 4):
            q_along_x(g, d).wait_send()
            y_copy(g, d).wait_send()
            for yy in range(NY):
                x_copy(g, d, yy).wait_send()
            for dx in range(NX):
                if (g, d, dx % 2) != (0, 1, 1):
                    q_along_y(g, dx, d).wait_send()
        for dz in range(1, NZ):
            z_copy(g, dz).wait_send()
    for dz in range(1, NZ):
        wo_copy(dz).wait_send()

    @pl.when(c != group)
    def _():
        wo_copy(0).wait_send()

    core_copy.wait()
    out_ref[...] = (mix[pl.ds(pl.multiple_of(c * 8, 8), 8), :] + mix_in[...]).astype(BF)


def local(context, latents, ends, w_query, w_key, w_value, w_out):
    dma = pltpu.SemaphoreType.DMA
    vmem = pltpu.VMEM
    hbm = pl.BlockSpec(memory_space=pl.ANY)
    return pl.pallas_call(
        kernel,
        out_shape=jax.ShapeDtypeStruct((8, 2 * FEAT), BF),
        in_specs=[hbm, hbm, pl.BlockSpec(memory_space=vmem), hbm, hbm, hbm, hbm],
        out_specs=pl.BlockSpec(memory_space=vmem),
        scratch_shapes=[
            vmem((POS, 1024), BF),
            vmem((ROWS, 1024), BF),
            vmem((1024, FEAT), BF),
            vmem((1024, FEAT), BF),
            vmem((1024, FEAT), BF),
            vmem((FEAT, 1024), BF),
            vmem((PHASES, NX * NY, WIDE, ROWS), BF),
            vmem((PHASES, POS, 128 * GROUP), BF),
            vmem((PHASES, VROWS * GROUP, POS), BF),
            vmem((PHASES, NX * NY, PAY, ROWS), BF),
            vmem((PHASES, 3, NY, PAY, ROWS), BF),
            vmem((PHASES, 3, PAY, ROWS), BF),
            vmem((PHASES, 3, PAY, ROWS), BF),
            vmem((PHASES, ROWS, WIDE + 128), BF),
            vmem((PHASES, NZ, OWN, WIDE + 128), BF),
            vmem((OWN, 1024), F32),
            vmem((8, 1024), F32),
            vmem((POS, 2 * ROWS), F32),
            dma((5,)), dma((2,)), dma((NZ,)), dma((HEADS,)),
            dma((PHASES, 3)), dma((2,)), dma((PHASES, NX, 3)), dma((PHASES, NX * NY)),
            dma((PHASES, 3, NY)), dma((PHASES, 3, NY)), dma((PHASES, 3)), dma((PHASES, 3)),
            dma((PHASES, NZ)), dma((PHASES, NZ)), dma((2,)),
        ],
        compiler_params=pltpu.CompilerParams(
            collective_id=0, has_side_effects=True, vmem_limit_bytes=63 * 2**20
        ),
        name="attend",
    )(context, latents, ends.reshape(NX * NY, ROWS), w_query, w_key, w_value, w_out)


def solution(mesh):
    in_specs = (P(("major", "minor"), None), P("major", None), P(), P(), P(), P(), P("minor", None))
    out_specs = P(("major", "minor"), None)
    return jax.shard_map(local, mesh=mesh, in_specs=in_specs, out_specs=out_specs, check_vma=False)
```

time: 1030 us -> 68.1 us (0.07); the launches traced: 1020 us -> 67.1 us
  waiting for transfers between devices: 664 us -> 0 us
  local copies, waits for them, and re-layouts: 216 us -> 1.32 us
  matrix products: 79.6 us -> 0 us
  Pallas kernels: 0 us -> 65.7 us
  other arithmetic: 43.2 us -> 0 us
  between operations: 13.6 us -> 0.01 us
    pmax x1 -> x0, waiting for transfers between devices: 237 us -> none  [local(): lax.pmax(block_max.astype(jnp.bfloat16), ('major', 'minor'))]
    reduce_scatter x3 -> x0, waiting for transfers between devices: 203 us -> none  [the longest x1 79.1 us: local(): lax.psum_scatter(by_heads[0], 'major', scatter_dimension=0, tiled=True)]
    dynamic_update_slice x24 -> x0, local copies, waits for them, and re-layouts: 179 us -> none  [local(): lax.map(one_block, (queries.reshape(nblocks, block_rows, heads, HEAD), li...]
    unnamed x9 -> x0, waiting for transfers between devices: 173 us -> none
    dot_general x12 -> x0, matrix products: 79.6 us -> none  [the longest x4 37.7 us: block_terms(): jnp.einsum('qhd,khd->qhk', query_block, key_heads, preferred_element_type...]
    pallas_call x0 -> x1, Pallas kernels: none -> 65.7 us  [local(): pl.pallas_call(kernel, out_shape=jax.ShapeDtypeStruct((8, 2 * FEAT), BF),...]
    all_gather x1 -> x0, waiting for transfers between devices: 51.2 us -> none  [local(): queries = lax.all_gather(own_queries, 'major', axis=0, tiled=True)]
    reduce_sum x4 -> x0, other arithmetic: 34.6 us -> none  [block_terms(): block_sum = jnp.sum(expon, axis=2)]
  transfers between devices with their start and end apart: 7 -> 0, of which waited for: 7 -> 0; matrix products, arithmetic and copies ran while one was open for 2% -> 0% of each run, Pallas kernels for 0% -> 0%
where the time goes in v1:
time: 68.1 us; the launch traced here: 67.1 us
  Pallas kernels  65.7 us (96%)
  local copies, waits for them, and re-layouts  1.32 us (2%)
    pallas_call x1, Pallas kernels, local(): pl.pallas_call(kernel, out_shape=jax.ShapeDtypeStruct((8, 2 * FEAT), BF),...  65.7 us

profile of v1, /device:TPU:17, one launch (start us, length us, event | category | flops | bytes accessed | tf_op | source)
XLA Modules:
  0.0 67.1 jit_solution(9121682178781065218)
XLA Ops:
  0.0 65.7 %attend.1 = bf16[8,1024]{1,0:T(8,128)(2,1)} custom-call(bf16[512,1024]{1,0:T(8,128)(2,1)} %ctx_ref.1, bf16[128,1024]{1,0:T(8,128)(2,1)} %lat_ref.1, s32[16,128]{1,0:T(8,128)} %bitcast.1, bf16[1024,1024]{1,0:T(8,128)(2,1)} %wq_ref.1, bf16[1024,1024]{1,0:T(8,128)(2,1)} %wk_ref.1, bf16[1024,1024]{1,0:T(8,128)(2,1)} %wv_ref.1, bf16[64,1024]{1,0:T(8,128)(2,1)} %wo_ref.1), custom_call_target="tpu_custom_call" | custom-call | tf_op jit(solution)/shard_map/attend/pallas_call | solution.py:434
  65.7 1.3 %copy.9 = bf16[8,1024]{1,0:T(8,128)(2,1)} copy(bf16[8,1024]{1,0:T(8,128)(2,1)} %attend.1) | data formatting | bytes 32768

commit v2 on v1

--- a/solution.py
+++ b/solution.py
@@ -17,6 +17,7 @@
 TOK = 512
 POS = 2 * TOK
 ROWS = 128
+PART = 128
 OWN = 2 * 8
 VROWS = 80
 PAY = WIDE + 32
@@ -67,7 +68,7 @@
 
 def kernel(
     ctx_ref, lat_ref, ends_ref, wq_ref, wk_ref, wv_ref, wo_ref, out_ref,
-    ctx, lat, wq, wk, wv, wo, qt, kk, vt, part, recv_x, sum_y, recv_y, zsend, zbuf, mix, mix_in, first_scores,
+    ctx, lat, wq, wk, wv, wo, qt, kk, vt, part, recv_x, sum_y, recv_y, zsend, zbuf, mix, mix_in, held, first_top,
     load_sem, ctx_sem, wo_send, wo_recv, qx_send, qd_send, qy_send, q_recv,
     x_send, x_recv, y_send, y_recv, z_send, z_recv, core_sem,
 ):
@@ -253,7 +254,7 @@
         zsend[g, :, :WIDE] = jnp.transpose(jnp.concatenate(nums, axis=0)).astype(BF)
         rows = jnp.concatenate([stats_rows(stats), jnp.zeros((96, ROWS), F32)], axis=0)
         zsend[g, :, WIDE:] = jnp.transpose(rows).astype(BF)
-        for dz in range(1, NZ):
+        for dz in (4, 3, 5, 2, 6, 1, 7):
             z_copy(g, dz).start()
         pltpu.make_async_copy(zsend.at[g, z_rows(0)], zbuf.at[g, z], z_recv.at[g, z]).start()
 
@@ -284,33 +285,42 @@
         pltpu.make_async_copy(wo_ref, wo.at[pl.ds(i * HEAD, HEAD)], wo_recv.at[i]).wait()
 
     base = (major * 16 + 2 * z) * TOK
-    place_in_pos = lax.broadcasted_iota(jnp.int32, (POS, 2 * ROWS), 0)
-
-    def scores(g, blocks, h):
+    place_in_part = lax.broadcasted_iota(jnp.int32, (PART, 2 * ROWS), 0)
+
+    def scores(g, blocks, h, slot):
+        ends = jnp.concatenate([ends_ref[pl.ds(b, 1), :] for b in blocks], axis=1) - base
         rows = slice(h * HEAD, h * HEAD + HEAD)
         qh = jnp.concatenate([qt[g, b, rows, :] for b in blocks], axis=1)
         qh = jnp.concatenate([qh, qh], axis=0)
-        return jnp.dot(kk[g, :, h * 128 : h * 128 + 128], qh, preferred_element_type=F32)
+        top = None
+        for j in range(0, POS, PART):
+            keys = kk[g, j : j + PART, h * 128 : h * 128 + 128]
+            now = jnp.dot(keys, qh, preferred_element_type=F32)
+            now = jnp.where(place_in_part < ends - j, now, NEG)
+            held[slot, j : j + PART, :] = now
+            most = jnp.max(now.reshape(PART // 8, 8, 2 * ROWS), axis=0)
+            top = most if top is None else jnp.maximum(top, most)
+        return jnp.ceil(jnp.max(top, axis=0, keepdims=True))
 
     def attend(g, blocks, next_g, next_blocks):
-        ends = jnp.concatenate([ends_ref[pl.ds(b, 1), :] for b in blocks], axis=1) - base
-        live = place_in_pos < ends
         tops, dens = [], []
-        ahead = first_scores[...]
+        top = first_top[...]
         for h in range(GROUP):
-            now = ahead
             if h + 1 < GROUP:
-                ahead = scores(g, blocks, h + 1)
+                next_top = scores(g, blocks, h + 1, (h + 1) % 2)
             else:
-                first_scores[...] = scores(next_g, next_blocks, 0)
-            now = jnp.where(live, now, NEG)
-            top = jnp.ceil(jnp.max(now, axis=0, keepdims=True))
-            probs = jnp.exp2(now - top).astype(BF)
+                next_top = scores(next_g, next_blocks, 0, 0)
+                first_top[...] = next_top
+            probs = [
+                jnp.exp2(held[h % 2, j : j + PART, :] - top).astype(BF) for j in range(0, POS, PART)
+            ]
+            probs = jnp.concatenate(probs, axis=0)
             res = jnp.dot(vt[g, h * VROWS : (h + 1) * VROWS, :], probs, preferred_element_type=F32)
             for i, b in enumerate(blocks):
                 part[g, b, h * HEAD : h * HEAD + HEAD, :] = res[:HEAD, i * ROWS : i * ROWS + ROWS].astype(BF)
             tops.append(top)
             dens.append(res[HEAD : HEAD + 1, :])
+            top = next_top
         rows = stats_rows(jnp.concatenate(tops + dens, axis=0)).astype(BF)
         for i, b in enumerate(blocks):
             part[g, b, WIDE:, :] = rows[:, i * ROWS : i * ROWS + ROWS]
@@ -388,7 +398,7 @@
         return carry
 
     q_wait(0, x, lax.rem(y + 1, NY))
-    first_scores[...] = scores(0, [own, q_block(x, lax.rem(y + 1, NY))], 0)
+    first_top[...] = scores(0, [own, q_block(x, lax.rem(y + 1, NY))], 0, 0)
     lax.fori_loop(0, 8 * PHASES, step, 0)
 
     add_along_x(1, 3)
@@ -454,7 +464,8 @@
             vmem((PHASES, NZ, OWN, WIDE + 128), BF),
             vmem((OWN, 1024), F32),
             vmem((8, 1024), F32),
-            vmem((POS, 2 * ROWS), F32),
+            vmem((2, POS, 2 * ROWS), F32),
+            vmem((1, 2 * ROWS), F32),
             dma((5,)), dma((2,)), dma((NZ,)), dma((HEADS,)),
             dma((PHASES, 3)), dma((2,)), dma((PHASES, NX, 3)), dma((PHASES, NX * NY)),
             dma((PHASES, 3, NY)), dma((PHASES, 3, NY)), dma((PHASES, 3)), dma((PHASES, 3)),

time: 68.1 us -> 66.1 us (0.971); the launches traced: 67.1 us -> 65.8 us
  Pallas kernels: 65.7 us -> 64.5 us
    pallas_call x1, Pallas kernels: 65.7 us -> 64.5 us  [local(): pl.pallas_call(kernel, out_shape=jax.ShapeDtypeStruct((8, 2 * FEAT), BF),...]
where the time goes in v2:
time: 66.1 us; the launch traced here: 65.8 us
  Pallas kernels  64.5 us (98%)
  local copies, waits for them, and re-layouts  1.32 us (2%)
    pallas_call x1, Pallas kernels, local(): pl.pallas_call(kernel, out_shape=jax.ShapeDtypeStruct((8, 2 * FEAT), BF),...  64.5 us
    unnamed x1, local copies, waits for them, and re-layouts  1.32 us

profile of v2, /device:TPU:17, one launch (start us, length us, event | category | flops | bytes accessed | tf_op | source)
XLA Modules:
  0.0 65.8 jit_solution(786544600963912936)
XLA Ops:
  0.0 64.5 %attend.1 = bf16[8,1024]{1,0:T(8,128)(2,1)} custom-call(bf16[512,1024]{1,0:T(8,128)(2,1)} %ctx_ref.1, bf16[128,1024]{1,0:T(8,128)(2,1)} %lat_ref.1, s32[16,128]{1,0:T(8,128)} %bitcast.1, bf16[1024,1024]{1,0:T(8,128)(2,1)} %wq_ref.1, bf16[1024,1024]{1,0:T(8,128)(2,1)} %wk_ref.1, bf16[1024,1024]{1,0:T(8,128)(2,1)} %wv_ref.1, bf16[64,1024]{1,0:T(8,128)(2,1)} %wo_ref.1), custom_call_target="tpu_custom_call" | custom-call | tf_op jit(solution)/shard_map/attend/pallas_call | solution.py:444
  64.5 1.3 %copy.9 = bf16[8,1024]{1,0:T(8,128)(2,1)} copy(bf16[8,1024]{1,0:T(8,128)(2,1)} %attend.1) | data formatting | bytes 32768

commit v3 on v2

--- a/solution.py
+++ b/solution.py
@@ -20,7 +20,7 @@
 PART = 128
 OWN = 2 * 8
 VROWS = 80
-PAY = WIDE + 32
+PAY = WIDE + 16
 LOG2E = math.log2(math.e)
 NEG = -1e30
 MESH = pl.DeviceIdType.MESH
@@ -38,12 +38,13 @@
 
 def stats_of(pay):
     rows = pay[WIDE:, :].astype(F32)
-    return rows[:8] + rows[8:16] + rows[16:24]
+    top = rows[:GROUP] + rows[GROUP : 2 * GROUP] + rows[2 * GROUP : 3 * GROUP]
+    return jnp.concatenate([top, rows[3 * GROUP :]], axis=0)
 
 
 def stats_rows(stats):
-    terms = [t.astype(F32) for t in split3(stats)]
-    return jnp.concatenate(terms + [jnp.zeros_like(stats)], axis=0)
+    terms = [t.astype(F32) for t in split3(stats[:GROUP])]
+    return jnp.concatenate(terms + [stats[GROUP:]], axis=0)
 
 
 def merge(pays):
@@ -109,13 +110,6 @@
             pl.semaphore_signal(barrier, inc=1, device_id=at_xy(d, e), device_id_type=MESH)
     for d in range(1, 16):
         pl.semaphore_signal(barrier, inc=1, device_id=(major, lax.rem(minor + d, 16)), device_id_type=MESH)
-    pl.semaphore_wait(barrier, 25)
-
-    ctx_copy = pltpu.make_async_remote_copy(
-        src_ref=ctx_ref, dst_ref=ctx.at[mine], send_sem=ctx_sem.at[0], recv_sem=ctx_sem.at[1],
-        device_id=other, device_id_type=MESH,
-    )
-    ctx_copy.start()
 
     def q_block(xx, yy):
         return xx * NY + yy
@@ -127,6 +121,13 @@
     q = jnp.transpose(q.astype(BF).astype(F32)).astype(BF)
     for g in range(PHASES):
         qt[g, own] = q[g * WIDE : (g + 1) * WIDE, :]
+
+    pl.semaphore_wait(barrier, 25)
+    ctx_copy = pltpu.make_async_remote_copy(
+        src_ref=ctx_ref, dst_ref=ctx.at[mine], send_sem=ctx_sem.at[0], recv_sem=ctx_sem.at[1],
+        device_id=other, device_id_type=MESH,
+    )
+    ctx_copy.start()
 
     def q_copy(g, block, send_sem, device):
         return pltpu.make_async_remote_copy(
@@ -252,7 +253,7 @@
             [part.at[g, own]] + [recv_x.at[g, d, y] for d in range(3)] + [recv_y.at[g, d] for d in range(3)]
         )
         zsend[g, :, :WIDE] = jnp.transpose(jnp.concatenate(nums, axis=0)).astype(BF)
-        rows = jnp.concatenate([stats_rows(stats), jnp.zeros((96, ROWS), F32)], axis=0)
+        rows = jnp.concatenate([stats_rows(stats), jnp.zeros((112, ROWS), F32)], axis=0)
         zsend[g, :, WIDE:] = jnp.transpose(rows).astype(BF)
         for dz in (4, 3, 5, 2, 6, 1, 7):
             z_copy(g, dz).start()
@@ -262,21 +263,19 @@
         head_of = lax.shift_right_logical(lax.broadcasted_iota(jnp.int32, (128, WIDE), 1), 6)
         line = lax.broadcasted_iota(jnp.int32, (128, WIDE), 0)
         spread = jnp.where(head_of == line, 1.0, 0.0).astype(BF)
-        spread_den = jnp.where(head_of == line - GROUP, 1.0, 0.0).astype(BF)
+        spread_den = jnp.where(head_of == line - 3 * GROUP, 1.0, 0.0).astype(BF)
         lane16 = lax.broadcasted_iota(jnp.int32, (OWN, 128), 1)
         for i in range(NZ):
             pltpu.make_async_copy(zsend.at[g, pl.ds(0, OWN)], zbuf.at[g, i], z_recv.at[g, i]).wait()
-        sums = []
-        for i in range(NZ):
-            t = zbuf[g, i, :, WIDE:].astype(F32)
-            sums.append(t + pltpu.roll(t, 120, 1) + pltpu.roll(t, 112, 1))
-        top = sums[0]
-        for t in sums[1:]:
+        sums = [zbuf[g, i, :, WIDE:].astype(F32) for i in range(NZ)]
+        tops = [t + pltpu.roll(t, 128 - GROUP, 1) + pltpu.roll(t, 128 - 2 * GROUP, 1) for t in sums]
+        top = tops[0]
+        for t in tops[1:]:
             top = jnp.maximum(top, t)
-        factors = [jnp.where(lane16 < GROUP, jnp.exp2(t - top), 0.0) for t in sums]
+        factors = [jnp.where(lane16 < GROUP, jnp.exp2(t - top), 0.0) for t in tops]
         wide = jnp.dot(jnp.concatenate(factors, axis=0).astype(BF), spread, preferred_element_type=F32)
         num = sum(wide[i * OWN : i * OWN + OWN] * zbuf[g, i, :, :WIDE].astype(F32) for i in range(NZ))
-        den = sum(pltpu.roll(f, GROUP, 1) * t for f, t in zip(factors, sums))
+        den = sum(pltpu.roll(f, 3 * GROUP, 1) * t for f, t in zip(factors, sums))
         den_wide = sum(jnp.dot(t, spread_den, preferred_element_type=F32) for t in split3(den))
         attended = (num / den_wide).astype(BF)
         return jnp.dot(attended, wo[g * WIDE : (g + 1) * WIDE, :], preferred_element_type=F32)

time: 66.1 us -> 64.8 us (0.980); the launches traced: 65.8 us -> 63.8 us
  Pallas kernels: 64.5 us -> 62.4 us
    pallas_call x1, Pallas kernels: 64.5 us -> 62.4 us  [local(): pl.pallas_call(kernel, out_shape=jax.ShapeDtypeStruct((8, 2 * FEAT), BF),...]
where the time goes in v3:
time: 64.8 us; the launch traced here: 63.8 us
  Pallas kernels  62.4 us (96%)
  local copies, waits for them, and re-layouts  1.32 us (2%)
    pallas_call x1, Pallas kernels, local(): pl.pallas_call(kernel, out_shape=jax.ShapeDtypeStruct((8, 2 * FEAT), BF),...  62.4 us
    unnamed x1, local copies, waits for them, and re-layouts  1.32 us

profile of v3, /device:TPU:17, one launch (start us, length us, event | category | flops | bytes accessed | tf_op | source)
XLA Modules:
  0.0 63.8 jit_solution(1005282106510668874)
XLA Ops:
  0.0 62.4 %attend.1 = bf16[8,1024]{1,0:T(8,128)(2,1)} custom-call(bf16[512,1024]{1,0:T(8,128)(2,1)} %ctx_ref.1, bf16[128,1024]{1,0:T(8,128)(2,1)} %lat_ref.1, s32[16,128]{1,0:T(8,128)} %bitcast.1, bf16[1024,1024]{1,0:T(8,128)(2,1)} %wq_ref.1, bf16[1024,1024]{1,0:T(8,128)(2,1)} %wk_ref.1, bf16[1024,1024]{1,0:T(8,128)(2,1)} %wv_ref.1, bf16[64,1024]{1,0:T(8,128)(2,1)} %wo_ref.1), custom_call_target="tpu_custom_call" | custom-call | tf_op jit(solution)/shard_map/attend/pallas_call | solution.py:443
  62.4 1.3 %copy.9 = bf16[8,1024]{1,0:T(8,128)(2,1)} copy(bf16[8,1024]{1,0:T(8,128)(2,1)} %attend.1) | data formatting | bytes 32768

commit v4 on v3

--- a/solution.py
+++ b/solution.py
@@ -355,17 +355,19 @@
                 q_wait(0, lax.rem(x + dx, NX), y)
                 for d in range(1 if dx == 2 else 2, 4):
                     q_along_y(0, dx, d).start()
+        @pl.when(it == 2)
+        def _():
             for d in (2, 1, 3):
                 q_along_x(1, d).start()
 
-        @pl.when(it == 3)
+        @pl.when(it == 4)
         def _():
             for dx in (2, 1, 3):
                 q_wait(1, lax.rem(x + dx, NX), y)
                 for d in range(1, 4):
                     q_along_y(1, dx, d).start()
 
-        @pl.when(it == 5)
+        @pl.when(it == 6)
         def _():
             for d in range(1, 4):
                 q_along_y(1, 0, d).start()

time: 64.8 us -> 64.9 us (level); the launches traced: 63.8 us -> 64.7 us
  Pallas kernels: 62.4 us -> 63.3 us
    pallas_call x1, Pallas kernels: 62.4 us -> 63.3 us  [local(): pl.pallas_call(kernel, out_shape=jax.ShapeDtypeStruct((8, 2 * FEAT), BF),...]
where the time goes in v4:
time: 64.9 us; the launch traced here: 64.7 us
  Pallas kernels  63.3 us (98%)
  local copies, waits for them, and re-layouts  1.32 us (2%)
    pallas_call x1, Pallas kernels, local(): pl.pallas_call(kernel, out_shape=jax.ShapeDtypeStruct((8, 2 * FEAT), BF),...  63.3 us
    unnamed x1, local copies, waits for them, and re-layouts  1.32 us

profile of v4, /device:TPU:17, one launch (start us, length us, event | category | flops | bytes accessed | tf_op | source)
XLA Modules:
  0.0 64.7 jit_solution(17784342727146502724)
XLA Ops:
  0.0 63.3 %attend.1 = bf16[8,1024]{1,0:T(8,128)(2,1)} custom-call(bf16[512,1024]{1,0:T(8,128)(2,1)} %ctx_ref.1, bf16[128,1024]{1,0:T(8,128)(2,1)} %lat_ref.1, s32[16,128]{1,0:T(8,128)} %bitcast.1, bf16[1024,1024]{1,0:T(8,128)(2,1)} %wq_ref.1, bf16[1024,1024]{1,0:T(8,128)(2,1)} %wk_ref.1, bf16[1024,1024]{1,0:T(8,128)(2,1)} %wv_ref.1, bf16[64,1024]{1,0:T(8,128)(2,1)} %wo_ref.1), custom_call_target="tpu_custom_call" | custom-call | tf_op jit(solution)/shard_map/attend/pallas_call | solution.py:445
  63.3 1.3 %copy.9 = bf16[8,1024]{1,0:T(8,128)(2,1)} copy(bf16[8,1024]{1,0:T(8,128)(2,1)} %attend.1) | data formatting | bytes 32768
